TPU v7x, 32 devices: a whole 2x2x4 slice. The times are simulated.
32 devices in a mesh: lon: 4 (over z), lat: 4 (over y, core), ch: 2 (over x).
Axes of the slice: x: 2, y: 2, z: 4, core: 2. Of those that a mesh axis runs over, the one named last changes fastest.
Arguments:
- state_field: bfloat16 [60, 720, 256], P('lat', 'lon', 'ch'), may hold values from -6 to 6
- cotangent: bfloat16 [60, 720, 256], P('lat', 'lon', 'ch'), may hold values from -6 to 6
- conv_kernel: float32 [2, 7, 7, 256], P(None, None, None, 'ch'), may hold values from -0.875 to 0.875
- conv_bias: float32 [2, 256], P(None, 'ch'), may hold values from -3 to 3
- norm_gain: float32 [2, 256], P(None, 'ch'), may hold values from 0.5 to 1.5
- weight_in: bfloat16 [2, 256, 1024], replicated, may hold values from -0.375 to 0.375
- bias_in: float32 [2, 1024], replicated, may hold values from -3 to 3
- weight_out: bfloat16 [2, 1024, 256], replicated, may hold values from -0.1875 to 0.1875
- layer_scale: float32 [2, 256], P(None, 'ch'), may hold values from 0.5 to 1.5
Outputs:
- gradient_field: float32 [60, 720, 256], P('lat', 'lon', 'ch')
All inputs are finite; a program needn't handle non-finite values.
Results may differ from a plain program's by a relative error of at most 0.0095.
Values may be sent and summed in bfloat16 or wider, within the bound.
A program may use at most 128 MiB of HBM per device.

v0:
```python
import functools

import jax
import jax.numpy as jnp
from jax import lax
from jax.experimental import pallas as pl
from jax.experimental.pallas import tpu as pltpu
from jax.sharding import PartitionSpec as P

GELU_SCALE = 0.7978845608028654
CUBIC_TERM = 0.044715
EPSILON = 1e-05
GROUP = 3
SPAN = 32
MESH = pl.DeviceIdType.MESH


def gelu_parts(preact):
    square = preact * preact
    tanh_term = jnp.tanh(GELU_SCALE * preact * (1.0 + CUBIC_TERM * square))
    rise = 0.5 * (1.0 + tanh_term)
    inner = GELU_SCALE * (1.0 + 3.0 * CUBIC_TERM * square)
    slope = rise + 0.5 * preact * (1.0 - tanh_term * tanh_term) * inner
    return preact * rise, slope


def matmul(left, right):
    return jnp.dot(left, right, preferred_element_type=jnp.float32)


def matmul_t(left, right):
    return lax.dot_general(
        left, right, (((1,), (1,)), ((), ())), preferred_element_type=jnp.float32
    )


def body(
    half,
    state_keep,
    state_send,
    cot_keep,
    cot_send,
    param_own,
    weight_in,
    bias_in,
    weight_out,
    out,
    fields,
    cot,
    param,
    edge_out,
    edge_in,
    shifts,
    smoothed,
    normed_kept,
    inverse_kept,
    slope_kept,
    gradient,
    parcel,
    landing,
    send_sem,
    recv_sem,
):
    rows, breadth, lanes = state_keep.shape
    groups = rows // GROUP
    hidden = weight_in.shape[2]
    chunk = hidden // 2
    lon, lat, ch = lax.axis_index("lon"), lax.axis_index("lat"), lax.axis_index("ch")
    lons, lats = lax.axis_size("lon"), lax.axis_size("lat")
    ring = lons * 2
    place = lon * 2 + ch
    north, south = lat == 0, lat == lats - 1
    right, left = lax.rem(place + 1, ring), lax.rem(place + ring - 1, ring)
    opposite = lax.rem(lon + lons // 2, lons)
    partner_id = {"lon": lon, "lat": lat, "ch": 1 - ch}
    right_id = {"lon": right // 2, "lat": lat, "ch": lax.rem(right, 2)}
    left_id = {"lon": left // 2, "lat": lat, "ch": lax.rem(left, 2)}
    up_id = {
        "lon": jnp.where(north, opposite, lon),
        "lat": jnp.where(north, lat, lat - 1),
        "ch": ch,
    }
    down_id = {
        "lon": jnp.where(south, opposite, lon),
        "lat": jnp.where(south, lat, lat + 1),
        "ch": ch,
    }

    def remote(source, target, slot, device, landing_slot=None):
        return pltpu.make_async_remote_copy(
            src_ref=source,
            dst_ref=target,
            send_sem=send_sem.at[slot],
            recv_sem=recv_sem.at[slot if landing_slot is None else landing_slot],
            device_id=device,
            device_id_type=MESH,
        )

    barrier = pltpu.get_barrier_semaphore()
    for device in (right_id, left_id, up_id, down_id):
        pl.semaphore_signal(barrier, inc=1, device_id=device, device_id_type=MESH)
    pl.semaphore_wait(barrier, 4)

    inner = pl.ds(3, rows)
    swaps = [
        remote(param_own, param.at[ch], 0, partner_id),
        remote(state_send, fields.at[0, ch, inner], 1, partner_id),
        remote(cot_send, cot.at[ch], 2, partner_id),
    ]
    for copy in swaps:
        copy.start()
    param[pl.ds(ch, 1)] = param_own[...][None]
    fields[0, pl.ds(ch, 1), inner] = state_keep[...][None]
    cot[pl.ds(ch, 1)] = cot_keep[...][None]
    swaps[0].wait()
    swaps[1].wait()

    spot = lax.broadcasted_iota(jnp.int32, (16, lanes), 0)
    last = breadth - 16
    first_right = half - last

    def turned(value, shift):
        shift = shift % value.shape[0]
        return value if shift == 0 else pltpu.roll(value, shift, 0)

    def send_edges(conv):
        for g in range(2):
            for k in range((rows + 3) // 4):
                packed = [None, None]
                for j in range(4):
                    row = 4 * k + j
                    if row < rows:
                        head = fields[conv, g, 3 + row, 0:16].astype(jnp.float32)
                        tail = fields[conv, g, 3 + row, last:breadth].astype(jnp.float32)
                        pieces = (
                            turned(head, 4 * j),
                            turned(tail, 4 * j - (first_right - 3)),
                        )
                        for way in range(2):
                            if packed[way] is None:
                                packed[way] = pieces[way]
                            else:
                                packed[way] = jnp.where(
                                    spot >= 4 * j, pieces[way], packed[way]
                                )
                for way in range(2):
                    edge_out[conv, way, g, k] = packed[way].astype(jnp.bfloat16)
        copies = [
            remote(edge_out.at[conv, way], edge_in.at[conv, way], 3 + 2 * conv + way, device)
            for way, device in ((0, left_id), (1, right_id))
        ]
        for copy in copies:
            copy.start()
        return copies

    def place_edges(conv):
        for g in range(2):
            for k in range((rows + 3) // 4):
                from_right = edge_in[conv, 0, g, k].astype(jnp.float32)
                from_left = edge_in[conv, 1, g, k].astype(jnp.float32)
                for j in range(4):
                    row = 4 * k + j
                    if row < rows:
                        tile = fields[conv, g, 3 + row, last:breadth].astype(jnp.float32)
                        tile = jnp.where(
                            spot >= first_right, turned(from_right, first_right - 4 * j), tile
                        )
                        tile = jnp.where(spot >= 13, turned(from_left, 13 - 4 * j), tile)
                        fields[conv, g, 3 + row, last:breadth] = tile.astype(jnp.bfloat16)

    def spread(conv, source, row):
        for g in range(2):
            line = fields[conv, g, source].astype(jnp.float32)
            for q in range(7):
                shifts[q, g, row] = turned(line, 3 - q)

    def convolve(conv, block, adjoint, write):
        for copy in send_edges(conv):
            copy.wait()
        place_edges(conv)
        base = 11 + 2 * conv
        upward = remote(
            fields.at[conv, :, pl.ds(3, 3)],
            fields.at[conv, :, pl.ds(jnp.where(north, 0, rows + 3), 3)],
            base,
            up_id,
            jnp.where(north, base, base + 1),
        )
        downward = remote(
            fields.at[conv, :, pl.ds(rows, 3)],
            fields.at[conv, :, pl.ds(jnp.where(south, rows + 3, 0), 3)],
            base + 1,
            down_id,
            jnp.where(south, base + 1, base),
        )
        upward.start()
        downward.start()

        def spread_row(row, carry):
            spread(conv, row + 3, row + 3)
            return carry

        lax.fori_loop(0, rows, spread_row, 0)

        def rows_of(group):
            top = (north & (group == 0)).astype(jnp.int32)
            bottom = (south & (group == groups - 1)).astype(jnp.int32)

            def piece(index, carry):
                g, part = index // (breadth // SPAN), lax.rem(index, breadth // SPAN)
                columns = pl.ds(pl.multiple_of(part * SPAN, SPAN), SPAN)
                sums = [jnp.zeros((SPAN, lanes), jnp.float32) for _ in range(GROUP)]
                for away in range(GROUP + 6):
                    mirror = top if away < 3 else bottom if away >= GROUP + 3 else None
                    for q in range(7):
                        line = shifts[q, g, GROUP * group + away, columns]
                        for i in range(GROUP):
                            p = away - i
                            if 0 <= p <= 6:
                                tap, across = p, q
                                if adjoint:
                                    tap, across = 6 - p, 6 - q
                                    if mirror is not None:
                                        tap = tap + mirror * (2 * p - 6)
                                weight = param[g, block * 7 + tap, across : across + 1]
                                sums[i] = sums[i] + line * weight
                for i in range(GROUP):
                    write(g, GROUP * group + i, columns, sums[i])
                return carry

            lax.fori_loop(0, 2 * (breadth // SPAN), piece, 0)

        def after(group):
            if conv == 3:
                send_rows(group)

        def middle_group(group, carry):
            rows_of(group)
            after(group)
            return carry

        lax.fori_loop(1, groups - 1, middle_group, 0)
        for slot, start in ((base, 0), (base + 1, rows + 3)):
            arrived = fields.at[conv, :, pl.ds(start, 3)]
            remote(arrived, arrived, slot, up_id).wait_recv()
        upward.wait_send()
        downward.wait_send()
        for k in range(3):
            spread(conv, jnp.where(north, 2 - k, k), k)
            spread(conv, jnp.where(south, rows + 5 - k, rows + 3 + k), rows + 3 + k)

        def end_group(index, carry):
            rows_of(index * (groups - 1))
            after(index * (groups - 1))
            return carry

        lax.fori_loop(0, 2, end_group, 0)

    def parcel_copy(group):
        lines = pl.ds(GROUP * group, GROUP)
        return remote(parcel.at[lines], landing.at[lines], 19 + group, partner_id)

    def send_rows(group):
        lines = pl.ds(GROUP * group, GROUP)
        parcel[lines] = gradient[pl.ds(1 - ch, 1), lines][0].astype(jnp.bfloat16)
        parcel_copy(group).start()

    def write_smoothed(g, row, columns, value):
        smoothed[g, row, columns] = value

    def write_gradient_one(g, row, columns, value):
        gradient[g, row, columns] = cot[g, row, columns].astype(jnp.float32) + value

    def write_gradient(g, row, columns, value):
        gradient[g, row, columns] = gradient[g, row, columns] + value

    def wide(ref, lines, *lead):
        parts = [
            ref[(*lead, g, lines)].astype(jnp.float32).reshape(GROUP * breadth, lanes)
            for g in range(2)
        ]
        return jnp.concatenate(parts, -1)

    def row_param(index):
        parts = [param[g, 14, index : index + 1] for g in range(2)]
        return jnp.concatenate(parts, -1)

    def store(conv, group, value):
        for g in range(2):
            part = value[:, g * lanes : (g + 1) * lanes].reshape(GROUP, breadth, lanes)
            fields[conv, g, pl.ds(3 + GROUP * group, GROUP)] = part

    def norm_of(group, block):
        value = wide(smoothed, pl.ds(GROUP * group, GROUP)) + row_param(block)
        average = jnp.mean(value, -1, keepdims=True)
        variance = jnp.mean(value * value, -1, keepdims=True) - average * average
        inverse_std = lax.rsqrt(variance + EPSILON)
        normed = (value - average) * inverse_std
        return normed, inverse_std, (normed * row_param(2 + block)).astype(jnp.bfloat16)

    def backward(grad_norm, normed, inverse_std, block):
        grad_scaled = grad_norm.astype(jnp.bfloat16).astype(jnp.float32) * row_param(2 + block)
        first_mean = jnp.mean(grad_scaled, -1, keepdims=True)
        second_mean = jnp.mean(grad_scaled * normed, -1, keepdims=True)
        return (inverse_std * (grad_scaled - first_mean - normed * second_mean)).astype(
            jnp.bfloat16
        )

    def spans():
        return [slice(k * chunk, (k + 1) * chunk) for k in range(2)]

    def first_forward(group, carry):
        normed, inverse_std, scaled = norm_of(group, 0)
        normed_kept[group] = normed
        inverse_kept[group] = inverse_std
        total = None
        for span in spans():
            preact = matmul(scaled, weight_in[0, :, span]) + bias_in[0:1, span]
            value, slope = gelu_parts(preact)
            slope_kept[group, :, span] = slope
            term = matmul(value.astype(jnp.bfloat16), weight_out[0, span])
            total = term if total is None else total + term
        mixed = total.astype(jnp.bfloat16).astype(jnp.float32)
        state = wide(fields, pl.ds(3 + GROUP * group, GROUP), 0)
        store(1, group, (state + row_param(4) * mixed).astype(jnp.bfloat16))
        return carry

    def second_both(group, carry):
        normed, inverse_std, scaled = norm_of(group, 1)
        grad_mix = (wide(cot, pl.ds(GROUP * group, GROUP)) * row_param(5)).astype(jnp.bfloat16)
        total = None
        for span in spans():
            preact = matmul(scaled, weight_in[1, :, span]) + bias_in[1:2, span]
            slope = gelu_parts(preact)[1]
            grad_act = (matmul_t(grad_mix, weight_out[1, span]) * slope).astype(jnp.bfloat16)
            term = matmul_t(grad_act, weight_in[1, :, span])
            total = term if total is None else total + term
        store(2, group, backward(total, normed, inverse_std, 1))
        return carry

    def first_backward(group, carry):
        grad_mix = (wide(gradient, pl.ds(GROUP * group, GROUP)) * row_param(4)).astype(
            jnp.bfloat16
        )
        total = None
        for span in spans():
            grad_hidden = matmul_t(grad_mix, weight_out[0, span])
            grad_act = (grad_hidden * slope_kept[group, :, span]).astype(jnp.bfloat16)
            term = matmul_t(grad_act, weight_in[0, :, span])
            total = term if total is None else total + term
        store(3, group, backward(total, normed_kept[group], inverse_kept[group], 0))
        return carry

    convolve(0, 0, False, write_smoothed)
    lax.fori_loop(0, groups, first_forward, 0)
    convolve(1, 1, False, write_smoothed)
    swaps[2].wait()
    lax.fori_loop(0, groups, second_both, 0)
    convolve(2, 1, True, write_gradient_one)
    lax.fori_loop(0, groups, first_backward, 0)
    convolve(3, 0, True, write_gradient)
    out[pl.ds(ch, 1)] = gradient[pl.ds(ch, 1)]
    for group in range(groups):
        parcel_copy(group).wait()
    out[pl.ds(1 - ch, 1)] = landing[...].astype(jnp.float32)[None]


def local(
    state_field,
    cotangent,
    conv_kernel,
    conv_bias,
    norm_gain,
    weight_in,
    bias_in,
    weight_out,
    layer_scale,
):
    first = lax.axis_index("ch") == 0
    rows, columns, lanes = state_field.shape
    half = columns // 2
    breadth = half + 6
    assert breadth % SPAN == 0 and rows % GROUP == 0 and lax.axis_size("ch") == 2

    def halves(field):
        parts = field[:, :half], field[:, half:]
        grow = ((0, 0), (0, breadth - half), (0, 0))
        return (
            jnp.pad(jnp.where(first, *parts), grow),
            jnp.pad(jnp.where(first, *parts[::-1]), grow),
        )

    taps = jnp.pad(conv_kernel, ((0, 0), (0, 0), (0, 1), (0, 0))).reshape(14, 8, lanes)
    rest = jnp.concatenate([conv_bias, norm_gain, layer_scale, layer_scale], 0)[None]
    param = jnp.concatenate([taps, rest], 0)
    groups = rows // GROUP
    hidden = weight_in.shape[2]
    cells = GROUP * breadth
    vmem = pl.BlockSpec(memory_space=pltpu.VMEM)
    result = pl.pallas_call(
        functools.partial(body, half),
        out_shape=jax.ShapeDtypeStruct((2, rows, breadth, lanes), jnp.float32),
        in_specs=[vmem] * 8,
        out_specs=vmem,
        scratch_shapes=[
            pltpu.VMEM((4, 2, rows + 6, breadth, lanes), jnp.bfloat16),
            pltpu.VMEM((2, rows, breadth, lanes), jnp.bfloat16),
            pltpu.VMEM((2, 15, 8, lanes), jnp.float32),
            pltpu.VMEM((4, 2, 2, (rows + 3) // 4, 16, lanes), jnp.bfloat16),
            pltpu.VMEM((4, 2, 2, (rows + 3) // 4, 16, lanes), jnp.bfloat16),
            pltpu.VMEM((7, 2, rows + 6, breadth, lanes), jnp.float32),
            pltpu.VMEM((2, rows, breadth, lanes), jnp.float32),
            pltpu.VMEM((groups, cells, 2 * lanes), jnp.float32),
            pltpu.VMEM((groups, cells, 1), jnp.float32),
            pltpu.VMEM((groups, cells, hidden), jnp.float32),
            pltpu.VMEM((2, rows, breadth, lanes), jnp.float32),
            pltpu.VMEM((rows, breadth, lanes), jnp.bfloat16),
            pltpu.VMEM((rows, breadth, lanes), jnp.bfloat16),
            pltpu.SemaphoreType.DMA((19 + groups,)),
            pltpu.SemaphoreType.DMA((19 + groups,)),
        ],
        compiler_params=pltpu.CompilerParams(
            collective_id=0, has_side_effects=True, vmem_limit_bytes=60 * 1024 * 1024
        ),
    )(*halves(state_field), *halves(cotangent), param, weight_in, bias_in, weight_out)
    return jnp.concatenate([result[0, :, :half], result[1, :, :half]], 1)


def solution(mesh):
    in_specs = (
        P("lat", "lon", "ch"),
        P("lat", "lon", "ch"),
        P(None, None, None, "ch"),
        P(None, "ch"),
        P(None, "ch"),
        P(),
        P(),
        P(),
        P(None, "ch"),
    )
    out_specs = P("lat", "lon", "ch")
    return jax.shard_map(local, mesh=mesh, in_specs=in_specs, out_specs=out_specs, check_vma=False)
```

profile of v0, /device:TPU:0, one launch (start us, length us, event | category | flops | bytes accessed | tf_op | source)
XLA Modules:
  0.0 101.9 jit_solution(13891473236745091275)
XLA Ops:
  0.0 0.8 maximum_bitcast_fusion
  0.8 0.8 copy.11
  1.6 0.6 pad_maximum_fusion.1.param_own
  2.2 1.5 %broadcast_select_fusion = (bf16[15,90,128]{2,1,0:T(8,128)(2,1)S(1)}, bf16[15,90,128]{2,1,0:T(8,128)(2,1)S(1)}, bf16[15,90,128]{2,1,0:T(8,128)(2,1)S(1)}, bf16[15,90,128]{2,1,0:T(8,128)(2,1)S(1)}) fusion(pred[]{:T(512)S(6)} %eq.3, bf16[15,180,128]{2,1,0:T(8,128)(2,1)} %param.10, bf16[15,180,128]{2,1,0:T(8,128)(2,1)} %param.9), kind=kLoop, calls=%fused_computation.3 | loop fusion | flops 691200 | bytes 2764801 | tf_op jit(solution)/shard_map/jit(_where)/select_n | solution.py:390
  3.8 0.8 pad.20.cot_send
  4.6 0.8 pad.19.cot_keep
  5.3 0.8 pad.17.state_keep
  6.1 0.8 pad.18.state_send
  6.9 92.4 %shard_map.91 = f32[2,15,96,128]{3,2,1,0:T(8,128)} custom-call(bf16[15,96,128]{2,1,0:T(8,128)(2,1)} %pad.17.state_keep, bf16[15,96,128]{2,1,0:T(8,128)(2,1)} %pad.18.state_send, bf16[15,96,128]{2,1,0:T(8,128)(2,1)} %pad.19.cot_keep, bf16[15,96,128]{2,1,0:T(8,128)(2,1)} %pad.20.cot_send, f32[15,8,128]{2,1,0:T(8,128)} %pad_maximum_fusion.1.param_own, ...), custom_call_target="tpu_custom_call" | custom-call | tf_op jit(solution)/shard_map/pallas_call | solution.py:400
  99.2 1.4 %slice_bitcast_fusion.1 = (f32[15,90,128]{2,1,0:T(8,128)S(1)}, f32[15,90,128]{2,1,0:T(8,128)S(1)}) fusion(f32[2,15,96,128]{3,2,1,0:T(8,128)} %shard_map.91), kind=kLoop, calls=%fused_computation.2 | loop fusion | bytes 2764800 | tf_op jit(solution)/shard_map/squeeze | solution.py:426
  100.7 1.2 %pad_maximum_fusion = f32[15,180,128]{2,1,0:T(8,128)} fusion(f32[15,90,128]{2,1,0:T(8,128)S(1)} %get-tuple-element.6, f32[15,90,128]{2,1,0:T(8,128)S(1)} %get-tuple-element.5), kind=kLoop, calls=%fused_computation | loop fusion | flops 345600 | bytes 2764800 | tf_op jit(solution)/shard_map/concatenate | solution.py:426
  (1 shorter events, 0.0 us)
where the time goes:
time: 102 us
  Pallas kernels  92.4 us (91%)
  local copies, waits for them, and re-layouts  5.35 us (5%)
  other arithmetic  4.13 us (4%)
    pallas_call x1, Pallas kernels, local(): pl.pallas_call(functools.partial(body, half), out_shape=jax.ShapeDtypeStr...  92.4 us

commit v1 on v0

--- a/solution.py
+++ b/solution.py
@@ -63,6 +63,10 @@
 ):
     rows, breadth, lanes = state_keep.shape
     groups = rows // GROUP
+    row_base = 2
+    state_base = row_base + 8
+    parcel_base = state_base + groups
+    edge_base = parcel_base + groups
     hidden = weight_in.shape[2]
     chunk = hidden // 2
     lon, lat, ch = lax.axis_index("lon"), lax.axis_index("lat"), lax.axis_index("ch")
@@ -104,16 +108,27 @@
     inner = pl.ds(3, rows)
     swaps = [
         remote(param_own, param.at[ch], 0, partner_id),
-        remote(state_send, fields.at[0, ch, inner], 1, partner_id),
-        remote(cot_send, cot.at[ch], 2, partner_id),
+        remote(cot_send, cot.at[ch], 1, partner_id),
     ]
-    for copy in swaps:
-        copy.start()
+
+    def state_swap(group):
+        lines = pl.ds(GROUP * group, GROUP)
+        return remote(
+            state_send.at[lines],
+            fields.at[0, ch, pl.ds(3 + GROUP * group, GROUP)],
+            state_base + group,
+            partner_id,
+        )
+
+    def order(step):
+        return jnp.where(step == 0, 0, jnp.where(step == 1, groups - 1, step - 1))
+
+    for step in range(groups):
+        state_swap(0 if step == 0 else groups - 1 if step == 1 else step - 1).start()
+    swaps[0].start()
     param[pl.ds(ch, 1)] = param_own[...][None]
     fields[0, pl.ds(ch, 1), inner] = state_keep[...][None]
     cot[pl.ds(ch, 1)] = cot_keep[...][None]
-    swaps[0].wait()
-    swaps[1].wait()
 
     spot = lax.broadcasted_iota(jnp.int32, (16, lanes), 0)
     last = breadth - 16
@@ -123,50 +138,88 @@
         shift = shift % value.shape[0]
         return value if shift == 0 else pltpu.roll(value, shift, 0)
 
-    def send_edges(conv):
-        for g in range(2):
-            for k in range((rows + 3) // 4):
-                packed = [None, None]
-                for j in range(4):
-                    row = 4 * k + j
-                    if row < rows:
-                        head = fields[conv, g, 3 + row, 0:16].astype(jnp.float32)
-                        tail = fields[conv, g, 3 + row, last:breadth].astype(jnp.float32)
-                        pieces = (
-                            turned(head, 4 * j),
-                            turned(tail, 4 * j - (first_right - 3)),
-                        )
-                        for way in range(2):
-                            if packed[way] is None:
-                                packed[way] = pieces[way]
-                            else:
-                                packed[way] = jnp.where(
-                                    spot >= 4 * j, pieces[way], packed[way]
-                                )
-                for way in range(2):
-                    edge_out[conv, way, g, k] = packed[way].astype(jnp.bfloat16)
-        copies = [
-            remote(edge_out.at[conv, way], edge_in.at[conv, way], 3 + 2 * conv + way, device)
+    def edge_copies(conv, group):
+        return [
+            remote(
+                edge_out.at[conv, way, group],
+                edge_in.at[conv, way, group],
+                edge_base + (2 * conv + way) * groups + group,
+                device,
+            )
             for way, device in ((0, left_id), (1, right_id))
         ]
-        for copy in copies:
+
+    def send_edges(conv, group):
+        for g in range(2):
+            packed = [None, None]
+            for j in range(GROUP):
+                row = 3 + GROUP * group + j
+                head = fields[conv, g, row, 0:16].astype(jnp.float32)
+                tail = fields[conv, g, row, last:breadth].astype(jnp.float32)
+                pieces = (
+                    turned(head, 4 * j),
+                    turned(tail, 4 * j - (first_right - 3)),
+                )
+                for way in range(2):
+                    if packed[way] is None:
+                        packed[way] = pieces[way]
+                    else:
+                        packed[way] = jnp.where(spot >= 4 * j, pieces[way], packed[way])
+            for way in range(2):
+                edge_out[conv, way, group, g] = packed[way].astype(jnp.bfloat16)
+        for copy in edge_copies(conv, group):
             copy.start()
-        return copies
-
-    def place_edges(conv):
+
+    def place_edges(conv, group):
+        for copy in edge_copies(conv, group):
+            copy.wait()
         for g in range(2):
-            for k in range((rows + 3) // 4):
-                from_right = edge_in[conv, 0, g, k].astype(jnp.float32)
-                from_left = edge_in[conv, 1, g, k].astype(jnp.float32)
-                for j in range(4):
-                    row = 4 * k + j
-                    if row < rows:
-                        tile = fields[conv, g, 3 + row, last:breadth].astype(jnp.float32)
-                        tile = jnp.where(
-                            spot >= first_right, turned(from_right, first_right - 4 * j), tile
-                        )
-                        tile = jnp.where(spot >= 13, turned(from_left, 13 - 4 * j), tile)
-                        fields[conv, g, 3 + row, last:breadth] = tile.astype(jnp.bfloat16)
+            from_right = edge_in[conv, 0, group, g].astype(jnp.float32)
+            from_left = edge_in[conv, 1, group, g].astype(jnp.float32)
+            for j in range(GROUP):
+                row = 3 + GROUP * group + j
+                tile = fields[conv, g, row, last:breadth].astype(jnp.float32)
+                tile = jnp.where(
+                    spot >= first_right, turned(from_right, first_right - 4 * j), tile
+                )
+                tile = jnp.where(spot >= 13, turned(from_left, 13 - 4 * j), tile)
+                fields[conv, g, row, last:breadth] = tile.astype(jnp.bfloat16)
+
+    def row_copies(conv):
+        base = row_base + 2 * conv
+        return (
+            remote(
+                fields.at[conv, :, pl.ds(3, 3)],
+                fields.at[conv, :, pl.ds(jnp.where(north, 0, rows + 3), 3)],
+                base,
+                up_id,
+                jnp.where(north, base, base + 1),
+            ),
+            remote(
+                fields.at[conv, :, pl.ds(rows, 3)],
+                fields.at[conv, :, pl.ds(jnp.where(south, rows + 3, 0), 3)],
+                base + 1,
+                down_id,
+                jnp.where(south, base + 1, base),
+            ),
+        )
+
+    def produce(conv, make):
+        def step_of(step, carry):
+            group = order(step)
+            make(group)
+            send_edges(conv, group)
+
+            @pl.when(step == 2)
+            def _():
+                place_edges(conv, 0)
+                place_edges(conv, groups - 1)
+                for copy in row_copies(conv):
+                    copy.start()
+
+            return carry
+
+        lax.fori_loop(0, groups, step_of, 0)
 
     def spread(conv, source, row):
         for g in range(2):
@@ -175,39 +228,27 @@
                 shifts[q, g, row] = turned(line, 3 - q)
 
     def convolve(conv, block, adjoint, write):
-        for copy in send_edges(conv):
-            copy.wait()
-        place_edges(conv)
-        base = 11 + 2 * conv
-        upward = remote(
-            fields.at[conv, :, pl.ds(3, 3)],
-            fields.at[conv, :, pl.ds(jnp.where(north, 0, rows + 3), 3)],
-            base,
-            up_id,
-            jnp.where(north, base, base + 1),
-        )
-        downward = remote(
-            fields.at[conv, :, pl.ds(rows, 3)],
-            fields.at[conv, :, pl.ds(jnp.where(south, rows + 3, 0), 3)],
-            base + 1,
-            down_id,
-            jnp.where(south, base + 1, base),
-        )
-        upward.start()
-        downward.start()
-
-        def spread_row(row, carry):
-            spread(conv, row + 3, row + 3)
-            return carry
-
-        lax.fori_loop(0, rows, spread_row, 0)
-
-        def rows_of(group):
+        def take_group(group, carry):
+            @pl.when((group > 0) & (group < groups - 1))
+            def _():
+                place_edges(conv, group)
+
+            def spread_row(row, inner_carry):
+                spread(conv, row, row)
+                return inner_carry
+
+            return lax.fori_loop(3 + GROUP * group, 3 + GROUP * (group + 1), spread_row, carry)
+
+        lax.fori_loop(0, groups, take_group, 0)
+
+        def rows_of(group, only=None):
             top = (north & (group == 0)).astype(jnp.int32)
             bottom = (south & (group == groups - 1)).astype(jnp.int32)
 
             def piece(index, carry):
                 g, part = index // (breadth // SPAN), lax.rem(index, breadth // SPAN)
+                if only is not None:
+                    g = only
                 columns = pl.ds(pl.multiple_of(part * SPAN, SPAN), SPAN)
                 sums = [jnp.zeros((SPAN, lanes), jnp.float32) for _ in range(GROUP)]
                 for away in range(GROUP + 6):
@@ -228,37 +269,53 @@
                     write(g, GROUP * group + i, columns, sums[i])
                 return carry
 
-            lax.fori_loop(0, 2 * (breadth // SPAN), piece, 0)
-
-        def after(group):
-            if conv == 3:
+            count = 2 if only is None else 1
+            lax.fori_loop(0, count * (breadth // SPAN), piece, 0)
+
+        firsts = 1 - ch if adjoint and block == 0 else None
+
+        def work(group, only, send):
+            rows_of(group, only)
+            if send:
                 send_rows(group)
 
-        def middle_group(group, carry):
-            rows_of(group)
-            after(group)
-            return carry
-
-        lax.fori_loop(1, groups - 1, middle_group, 0)
+        def middle(only, send):
+            def step(group, carry):
+                work(group, only, send)
+                return carry
+
+            lax.fori_loop(1, groups - 1, step, 0)
+
+        def ends(only, send):
+            def step(index, carry):
+                work(index * (groups - 1), only, send)
+                return carry
+
+            lax.fori_loop(0, 2, step, 0)
+
+        middle(firsts, firsts is not None)
+        base = row_base + 2 * conv
         for slot, start in ((base, 0), (base + 1, rows + 3)):
             arrived = fields.at[conv, :, pl.ds(start, 3)]
             remote(arrived, arrived, slot, up_id).wait_recv()
-        upward.wait_send()
-        downward.wait_send()
+        for copy in row_copies(conv):
+            copy.wait_send()
+        if conv == 0:
+            swaps[1].start()
         for k in range(3):
             spread(conv, jnp.where(north, 2 - k, k), k)
             spread(conv, jnp.where(south, rows + 5 - k, rows + 3 + k), rows + 3 + k)
-
-        def end_group(index, carry):
-            rows_of(index * (groups - 1))
-            after(index * (groups - 1))
-            return carry
-
-        lax.fori_loop(0, 2, end_group, 0)
+        ends(firsts, firsts is not None)
+        if firsts is not None:
+            def own_step(group, carry):
+                rows_of(group, ch)
+                return carry
+
+            lax.fori_loop(0, groups, own_step, 0)
 
     def parcel_copy(group):
         lines = pl.ds(GROUP * group, GROUP)
-        return remote(parcel.at[lines], landing.at[lines], 19 + group, partner_id)
+        return remote(parcel.at[lines], landing.at[lines], parcel_base + group, partner_id)
 
     def send_rows(group):
         lines = pl.ds(GROUP * group, GROUP)
@@ -309,7 +366,7 @@
     def spans():
         return [slice(k * chunk, (k + 1) * chunk) for k in range(2)]
 
-    def first_forward(group, carry):
+    def first_forward(group):
         normed, inverse_std, scaled = norm_of(group, 0)
         normed_kept[group] = normed
         inverse_kept[group] = inverse_std
@@ -323,9 +380,8 @@
         mixed = total.astype(jnp.bfloat16).astype(jnp.float32)
         state = wide(fields, pl.ds(3 + GROUP * group, GROUP), 0)
         store(1, group, (state + row_param(4) * mixed).astype(jnp.bfloat16))
-        return carry
-
-    def second_both(group, carry):
+
+    def second_both(group):
         normed, inverse_std, scaled = norm_of(group, 1)
         grad_mix = (wide(cot, pl.ds(GROUP * group, GROUP)) * row_param(5)).astype(jnp.bfloat16)
         total = None
@@ -336,9 +392,8 @@
             term = matmul_t(grad_act, weight_in[1, :, span])
             total = term if total is None else total + term
         store(2, group, backward(total, normed, inverse_std, 1))
-        return carry
-
-    def first_backward(group, carry):
+
+    def first_backward(group):
         grad_mix = (wide(gradient, pl.ds(GROUP * group, GROUP)) * row_param(4)).astype(
             jnp.bfloat16
         )
@@ -349,15 +404,16 @@
             term = matmul_t(grad_act, weight_in[0, :, span])
             total = term if total is None else total + term
         store(3, group, backward(total, normed_kept[group], inverse_kept[group], 0))
-        return carry
-
+
+    produce(0, lambda group: state_swap(group).wait())
+    swaps[0].wait()
     convolve(0, 0, False, write_smoothed)
-    lax.fori_loop(0, groups, first_forward, 0)
+    produce(1, first_forward)
     convolve(1, 1, False, write_smoothed)
-    swaps[2].wait()
-    lax.fori_loop(0, groups, second_both, 0)
+    swaps[1].wait()
+    produce(2, second_both)
     convolve(2, 1, True, write_gradient_one)
-    lax.fori_loop(0, groups, first_backward, 0)
+    produce(3, first_backward)
     convolve(3, 0, True, write_gradient)
     out[pl.ds(ch, 1)] = gradient[pl.ds(ch, 1)]
     for group in range(groups):
@@ -406,8 +462,8 @@
             pltpu.VMEM((4, 2, rows + 6, breadth, lanes), jnp.bfloat16),
             pltpu.VMEM((2, rows, breadth, lanes), jnp.bfloat16),
             pltpu.VMEM((2, 15, 8, lanes), jnp.float32),
-            pltpu.VMEM((4, 2, 2, (rows + 3) // 4, 16, lanes), jnp.bfloat16),
-            pltpu.VMEM((4, 2, 2, (rows + 3) // 4, 16, lanes), jnp.bfloat16),
+            pltpu.VMEM((4, 2, groups, 2, 16, lanes), jnp.bfloat16),
+            pltpu.VMEM((4, 2, groups, 2, 16, lanes), jnp.bfloat16),
             pltpu.VMEM((7, 2, rows + 6, breadth, lanes), jnp.float32),
             pltpu.VMEM((2, rows, breadth, lanes), jnp.float32),
             pltpu.VMEM((groups, cells, 2 * lanes), jnp.float32),
@@ -416,8 +472,8 @@
             pltpu.VMEM((2, rows, breadth, lanes), jnp.float32),
             pltpu.VMEM((rows, breadth, lanes), jnp.bfloat16),
             pltpu.VMEM((rows, breadth, lanes), jnp.bfloat16),
-            pltpu.SemaphoreType.DMA((19 + groups,)),
-            pltpu.SemaphoreType.DMA((19 + groups,)),
+            pltpu.SemaphoreType.DMA((10 + 10 * groups,)),
+            pltpu.SemaphoreType.DMA((10 + 10 * groups,)),
         ],
         compiler_params=pltpu.CompilerParams(
             collective_id=0, has_side_effects=True, vmem_limit_bytes=60 * 1024 * 1024

time: 102 us -> 102 us (level)
  no operation moved by 1% of the time
where the time goes in v1:
time: 102 us
  Pallas kernels  92.1 us (90%)
  local copies, waits for them, and re-layouts  5.35 us (5%)
  other arithmetic  4.13 us (4%)
    pallas_call x1, Pallas kernels, local(): pl.pallas_call(functools.partial(body, half), out_shape=jax.ShapeDtypeStr...  92.1 us

profile of v1, /device:TPU:0, one launch (start us, length us, event | category | flops | bytes accessed | tf_op | source)
XLA Modules:
  0.0 101.6 jit_solution(17885047885005706568)
XLA Ops:
  0.0 0.8 maximum_bitcast_fusion
  0.8 0.8 copy.11
  1.6 0.6 pad_maximum_fusion.1.param_own
  2.2 1.5 %broadcast_select_fusion = (bf16[15,90,128]{2,1,0:T(8,128)(2,1)S(1)}, bf16[15,90,128]{2,1,0:T(8,128)(2,1)S(1)}, bf16[15,90,128]{2,1,0:T(8,128)(2,1)S(1)}, bf16[15,90,128]{2,1,0:T(8,128)(2,1)S(1)}) fusion(pred[]{:T(512)S(6)} %eq.3, bf16[15,180,128]{2,1,0:T(8,128)(2,1)} %param.10, bf16[15,180,128]{2,1,0:T(8,128)(2,1)} %param.9), kind=kLoop, calls=%fused_computation.3 | loop fusion | flops 691200 | bytes 2764801 | tf_op jit(solution)/shard_map/jit(_where)/select_n | solution.py:446
  3.8 0.8 pad.20.cot_send
  4.6 0.8 pad.19.cot_keep
  5.3 0.8 pad.17.state_keep
  6.1 0.8 pad.18.state_send
  6.9 92.1 %shard_map.91 = f32[2,15,96,128]{3,2,1,0:T(8,128)} custom-call(bf16[15,96,128]{2,1,0:T(8,128)(2,1)} %pad.17.state_keep, bf16[15,96,128]{2,1,0:T(8,128)(2,1)} %pad.18.state_send, bf16[15,96,128]{2,1,0:T(8,128)(2,1)} %pad.19.cot_keep, bf16[15,96,128]{2,1,0:T(8,128)(2,1)} %pad.20.cot_send, f32[15,8,128]{2,1,0:T(8,128)} %pad_maximum_fusion.1.param_own, ...), custom_call_target="tpu_custom_call" | custom-call | tf_op jit(solution)/shard_map/pallas_call | solution.py:456
  99.0 1.4 %slice_bitcast_fusion.1 = (f32[15,90,128]{2,1,0:T(8,128)S(1)}, f32[15,90,128]{2,1,0:T(8,128)S(1)}) fusion(f32[2,15,96,128]{3,2,1,0:T(8,128)} %shard_map.91), kind=kLoop, calls=%fused_computation.2 | loop fusion | bytes 2764800 | tf_op jit(solution)/shard_map/squeeze | solution.py:482
  100.4 1.2 %pad_maximum_fusion = f32[15,180,128]{2,1,0:T(8,128)} fusion(f32[15,90,128]{2,1,0:T(8,128)S(1)} %get-tuple-element.6, f32[15,90,128]{2,1,0:T(8,128)S(1)} %get-tuple-element.5), kind=kLoop, calls=%fused_computation | loop fusion | flops 345600 | bytes 2764800 | tf_op jit(solution)/shard_map/concatenate | solution.py:482
  (1 shorter events, 0.0 us)

commit v2 on v1

--- a/solution.py
+++ b/solution.py
@@ -439,12 +439,10 @@
     assert breadth % SPAN == 0 and rows % GROUP == 0 and lax.axis_size("ch") == 2
 
     def halves(field):
-        parts = field[:, :half], field[:, half:]
-        grow = ((0, 0), (0, breadth - half), (0, 0))
-        return (
-            jnp.pad(jnp.where(first, *parts), grow),
-            jnp.pad(jnp.where(first, *parts[::-1]), grow),
-        )
+        zero = jnp.zeros((), field.dtype)
+        low = field[:, :breadth]
+        high = lax.pad(field, zero, ((0, 0, 0), (-half, breadth - half, 0), (0, 0, 0)))
+        return jnp.where(first, low, high), jnp.where(first, high, low)
 
     taps = jnp.pad(conv_kernel, ((0, 0), (0, 0), (0, 1), (0, 0))).reshape(14, 8, lanes)
     rest = jnp.concatenate([conv_bias, norm_gain, layer_scale, layer_scale], 0)[None]

time: 102 us -> 101 us (level)
  local copies, waits for them, and re-layouts: 5.35 us -> 2.26 us
  other arithmetic: 4.13 us -> 5.94 us
    pad x4 -> x0, local copies, waits for them, and re-layouts: 3.1 us -> none  [the longest x2 1.55 us: halves(): jnp.pad(jnp.where(first, *parts[::-1]), grow)]
    select_n x1, other arithmetic: 1.54 us -> 3.35 us  [halves(): return (jnp.where(first, low, high), jnp.where(first, high, low))]
where the time goes in v2:
time: 101 us; the launch traced here: 100 us
  Pallas kernels  92.1 us (91%)
  other arithmetic  5.94 us (6%)
  local copies, waits for them, and re-layouts  2.26 us (2%)
    pallas_call x1, Pallas kernels, local(): pl.pallas_call(functools.partial(body, half), out_shape=jax.ShapeDtypeStr...  92.1 us
    select_n x1, other arithmetic, halves(): return (jnp.where(first, low, high), jnp.where(first, high, low))  3.35 us

profile of v2, /device:TPU:0, one launch (start us, length us, event | category | flops | bytes accessed | tf_op | source)
XLA Modules:
  0.0 100.3 jit_solution(4325522813733485348)
XLA Ops:
  0.0 0.8 maximum_bitcast_fusion
  0.8 0.8 copy.11
  1.6 0.6 pad_maximum_fusion.1.param_own
  2.2 3.3 %broadcast_select_fusion = (bf16[15,96,128]{2,1,0:T(8,128)(2,1)}, bf16[15,96,128]{2,1,0:T(8,128)(2,1)}, bf16[15,96,128]{2,1,0:T(8,128)(2,1)}, bf16[15,96,128]{2,1,0:T(8,128)(2,1)}) fusion(pred[]{:T(512)S(6)} %eq.3, bf16[15,180,128]{2,1,0:T(8,128)(2,1)} %param.10, bf16[15,180,128]{2,1,0:T(8,128)(2,1)} %param.9), kind=kLoop, calls=%fused_computation.5 | loop fusion | flops 737280 | bytes 3624961 | tf_op jit(solution)/shard_map/jit(_where)/select_n | solution.py:445
  5.6 92.1 %shard_map.91 = f32[2,15,96,128]{3,2,1,0:T(8,128)} custom-call(bf16[15,96,128]{2,1,0:T(8,128)(2,1)} %get-tuple-element.11.state_keep, bf16[15,96,128]{2,1,0:T(8,128)(2,1)} %get-tuple-element.12.state_send, bf16[15,96,128]{2,1,0:T(8,128)(2,1)} %get-tuple-element.8.cot_keep, bf16[15,96,128]{2,1,0:T(8,128)(2,1)} %get-tuple-element.7.cot_send, ...), custom_call_target="tpu_custom_call" | custom-call | tf_op jit(solution)/shard_map/pallas_call | solution.py:454
  97.7 1.4 %slice_bitcast_fusion.1 = (f32[15,90,128]{2,1,0:T(8,128)S(1)}, f32[15,90,128]{2,1,0:T(8,128)S(1)}) fusion(f32[2,15,96,128]{3,2,1,0:T(8,128)} %shard_map.91), kind=kLoop, calls=%fused_computation.2 | loop fusion | bytes 2764800 | tf_op jit(solution)/shard_map/squeeze | solution.py:480
  99.1 1.2 %pad_maximum_fusion = f32[15,180,128]{2,1,0:T(8,128)} fusion(f32[15,90,128]{2,1,0:T(8,128)S(1)} %get-tuple-element.6, f32[15,90,128]{2,1,0:T(8,128)S(1)} %get-tuple-element.5), kind=kLoop, calls=%fused_computation | loop fusion | flops 345600 | bytes 2764800 | tf_op jit(solution)/shard_map/concatenate | solution.py:480
  (1 shorter events, 0.0 us)
